TPU v7x, 32 devices: a whole 2x2x4 slice. The times are simulated.
32 devices in a mesh: seq: 8 (over y, x, core), chan: 4 (over z).
Axes of the slice: x: 2, y: 2, z: 4, core: 2. Of those that a mesh axis runs over, the one named last changes fastest.
Arguments:
- gate_in: bfloat16 [4096, 1024], P('seq', 'chan'), may hold values from -6 to 6
- out_gate: bfloat16 [4096, 1024], P('seq', 'chan'), may hold values from -6 to 6
- value_in: bfloat16 [4096, 1024], P('seq', 'chan'), may hold values from -6 to 6
- out_grad: bfloat16 [4096, 1024], P('seq', 'chan'), may hold values from -6 to 6
- skip_gain: float32 [1024], P('chan'), may hold values from -1 to 1
- filter_taps: float32 [4096, 256], P('seq'), may hold values from -0.09375 to 0.09375
Outputs:
- grad_gate: bfloat16 [4096, 1024], P('seq', 'chan')
- grad_out_gate: bfloat16 [4096, 1024], P('seq', 'chan')
- grad_value: bfloat16 [4096, 1024], P('seq', 'chan')
- skip_grad: float32 [1024], P('chan')
- taps_grad: float32 [4096, 256], P('seq')
All inputs are finite; a program needn't handle non-finite values.
Results may differ from a plain program's by a relative error of at most 0.0052.
Values sent between devices are 32-bit elements; how exact they have to be, the bound alone decides.
A program may use at most 128 MiB of HBM per device.

v0:
```python
import math

import jax
import jax.numpy as jnp
from jax import lax
from jax.sharding import PartitionSpec as P

HIGHEST = lax.Precision.HIGHEST


def angle_table(row_count, col_count, period, row_offset):
    row_ids = lax.iota(jnp.int32, row_count)[:, None] + row_offset
    col_ids = lax.iota(jnp.int32, col_count)[None, :]
    phase_turns = row_ids * col_ids % period
    phase_angle = phase_turns.astype(jnp.float32) * (2.0 * math.pi / period)
    return (jnp.cos(phase_angle), jnp.sin(phase_angle))


def split_length(count):
    best_factor = 1
    for candidate in range(1, math.isqrt(count) + 1):
        if count % candidate == 0:
            best_factor = candidate
    return best_factor


def dft_axis(x_re, x_im, axis, sign):
    count = x_re.shape[axis]
    first = split_length(count)
    second = count // first
    moved_re = jnp.moveaxis(x_re, axis, 0)
    moved_im = jnp.moveaxis(x_im, axis, 0)
    trailing = moved_re.shape[1:]
    moved_re = moved_re.reshape((first, second) + trailing)
    moved_im = moved_im.reshape((first, second) + trailing)
    cos_a, sin_a = angle_table(first, first, first, 0)
    step_re = jnp.einsum("kj,jb...->kb...", cos_a, moved_re, precision=HIGHEST) - sign * jnp.einsum(
        "kj,jb...->kb...", sin_a, moved_im, precision=HIGHEST
    )
    step_im = jnp.einsum("kj,jb...->kb...", cos_a, moved_im, precision=HIGHEST) + sign * jnp.einsum(
        "kj,jb...->kb...", sin_a, moved_re, precision=HIGHEST
    )
    cos_t, sin_t = angle_table(first, second, count, 0)
    cos_t = cos_t.reshape((first, second) + (1,) * len(trailing))
    sin_t = sin_t.reshape((first, second) + (1,) * len(trailing))
    turned_re = step_re * cos_t - sign * step_im * sin_t
    turned_im = step_im * cos_t + sign * step_re * sin_t
    cos_b, sin_b = angle_table(second, second, second, 0)
    final_re = jnp.einsum(
        "mb,kb...->mk...", cos_b, turned_re, precision=HIGHEST
    ) - sign * jnp.einsum("mb,kb...->mk...", sin_b, turned_im, precision=HIGHEST)
    final_im = jnp.einsum(
        "mb,kb...->mk...", cos_b, turned_im, precision=HIGHEST
    ) + sign * jnp.einsum("mb,kb...->mk...", sin_b, turned_re, precision=HIGHEST)
    final_re = jnp.moveaxis(final_re.reshape((count,) + trailing), 0, axis)
    final_im = jnp.moveaxis(final_im.reshape((count,) + trailing), 0, axis)
    return (final_re, final_im)


def spectral_products(spectra):
    mixed_re, mixed_im = (spectra[0, 0], spectra[0, 1])
    gated_re, gated_im = (spectra[1, 0], spectra[1, 1])
    filt_re, filt_im = (spectra[2, 0], spectra[2, 1])
    conv_pair = jnp.stack(
        [filt_re * mixed_re - filt_im * mixed_im, filt_re * mixed_im + filt_im * mixed_re]
    )
    corr_pair = jnp.stack(
        [gated_re * filt_re + gated_im * filt_im, gated_im * filt_re - gated_re * filt_im]
    )
    grad_pair = jnp.stack(
        [gated_re * mixed_re + gated_im * mixed_im, gated_im * mixed_re - gated_re * mixed_im]
    )
    return jnp.stack([conv_pair, corr_pair, grad_pair])


def body(gate_in, out_gate, value_in, out_grad, skip_gain, filter_taps):
    shards = lax.axis_size("seq")
    shard_id = lax.axis_index("seq")
    seq_rows, channel_count = gate_in.shape
    part_rows = seq_rows // shards
    length_all = 2 * shards * seq_rows
    mixed_bf = lax.optimization_barrier(
        (gate_in.astype(jnp.float32) * value_in.astype(jnp.float32)).astype(jnp.bfloat16)
    )
    gated_bf = lax.optimization_barrier(
        (out_grad.astype(jnp.float32) * out_gate.astype(jnp.float32)).astype(jnp.bfloat16)
    )
    mixed_f32 = mixed_bf.astype(jnp.float32)
    gated_f32 = gated_bf.astype(jnp.float32)
    stacked_rows = jnp.stack([mixed_f32, gated_f32])
    pair_rows = stacked_rows.reshape(2, shards, part_rows, channel_count)
    moved_pair, moved_filter = (
        lax.all_to_all(pair_rows, "seq", split_axis=1, concat_axis=1, tiled=True),
        lax.all_to_all(
            filter_taps.reshape(1, shards, part_rows, channel_count),
            "seq",
            split_axis=1,
            concat_axis=1,
            tiled=True,
        ),
    )
    fields = jnp.concatenate([moved_pair, moved_filter], axis=0)
    cos_pr, sin_pr = angle_table(2 * shards, shards, 2 * shards, 0)
    rows_re = jnp.einsum("rp,apjc->arjc", cos_pr, fields, precision=HIGHEST)
    rows_im = -jnp.einsum("rp,apjc->arjc", sin_pr, fields, precision=HIGHEST)
    cos_tw, sin_tw = angle_table(part_rows, 2 * shards, length_all, shard_id * part_rows)
    cos_tw = cos_tw.T[None, :, :, None]
    sin_tw = sin_tw.T[None, :, :, None]
    twisted = jnp.stack(
        [rows_re * cos_tw + rows_im * sin_tw, rows_im * cos_tw - rows_re * sin_tw], axis=1
    )
    columns = lax.all_to_all(twisted, "seq", split_axis=2, concat_axis=3, tiled=True)
    out_re, out_im = dft_axis(columns[:, 0], columns[:, 1], 2, -1.0)
    spectra = jnp.stack([out_re, out_im], axis=1)
    blocks = lax.all_to_all(spectra, "seq", split_axis=3, concat_axis=2, tiled=True)
    mixed_spec = lax.all_to_all(
        spectral_products(blocks), "seq", split_axis=2, concat_axis=3, tiled=True
    )
    back_re, back_im = dft_axis(mixed_spec[:, 0], mixed_spec[:, 1], 2, 1.0)
    back_cols = jnp.stack([back_re, back_im], axis=1)
    cos_pp, sin_pp = angle_table(shards, 2 * shards, 2 * shards, 0)
    gathered = lax.all_to_all(back_cols, "seq", split_axis=3, concat_axis=2, tiled=True)
    part_re = gathered[:, 0]
    part_im = gathered[:, 1]
    turned_re = part_re * cos_tw - part_im * sin_tw
    turned_im = part_im * cos_tw + part_re * sin_tw
    summed = jnp.einsum("pr,arjc->apjc", cos_pp, turned_re, precision=HIGHEST) - jnp.einsum(
        "pr,arjc->apjc", sin_pp, turned_im, precision=HIGHEST
    )
    results = summed * (1.0 / length_all)
    natural = lax.all_to_all(results, "seq", split_axis=1, concat_axis=1, tiled=True).reshape(
        3, seq_rows, channel_count
    )
    conv_out, corr_out, filt_grad = (natural[0], natural[1], natural[2])
    taps_grad = lax.psum(filt_grad, "chan")
    out_f32 = out_grad.astype(jnp.float32)
    grad_out_gate = (out_f32 * (conv_out + skip_gain[None] * mixed_f32)).astype(jnp.bfloat16)
    mix_grad = corr_out + skip_gain[None] * gated_f32
    grad_gate = (mix_grad * value_in.astype(jnp.float32)).astype(jnp.bfloat16)
    grad_value = (mix_grad * gate_in.astype(jnp.float32)).astype(jnp.bfloat16)
    skip_grad = lax.psum(jnp.sum(gated_f32 * mixed_f32, axis=0), "seq")
    return (grad_gate, grad_out_gate, grad_value, skip_grad, taps_grad)


def solution(mesh):
    placed = (
        P("seq", "chan"),
        P("seq", "chan"),
        P("seq", "chan"),
        P("seq", "chan"),
        P("chan"),
        P("seq", None),
    )
    return jax.shard_map(
        body,
        mesh=mesh,
        in_specs=placed,
        out_specs=(P("seq", "chan"), P("seq", "chan"), P("seq", "chan"), P("chan"), P("seq", None)),
        check_vma=False,
    )
```

profile of v0, /device:TPU:0, one launch (start us, length us, event | category | flops | bytes accessed | tf_op | source)
XLA Modules:
  0.0 584.4 jit_solution(14443220933125642228)
XLA Ops:
  7.2 1.1 fusion.73
  8.3 1.1 fusion.71
  9.4 0.7 copy-done
  10.3 1.1 copy.84
  11.3 5.2 all-to-all-start
  16.5 15.4 %all-to-all-done = f32[2,8,64,256]{3,2,0,1:T(8,128)S(1)} async-done(((f32[2,8,64,256]{3,2,0,1:T(8,128)}), f32[2,8,64,256]{3,2,0,1:T(8,128)S(1)}, u32[]{:S(2)}, u32[]{:S(2)}) %all-to-all-start) | async-done | bytes 1048608 | tf_op jit(solution)/shard_map/all_to_all | solution.py:93
  31.9 4.2 all-to-all-start.1
  36.3 0.6 copy_dynamic-update-slice_fusion
  36.9 8.9 %all-to-all-done.1 = f32[1,8,64,256]{3,2,0,1:T(8,128)} async-done(((f32[1,8,64,256]{3,2,0,1:T(8,128)}), f32[1,8,64,256]{3,2,0,1:T(8,128)}, u32[]{:S(2)}, u32[]{:S(2)}) %all-to-all-start.1) | async-done | bytes 524320 | tf_op jit(solution)/shard_map/all_to_all | solution.py:94
  45.8 1.3 copy_dynamic-update-slice_fusion.1
  47.2 2.8 fusion.137
  50.0 3.7 fusion.1
  53.7 1.4 pad_maximum_fusion
  55.1 6.3 %copy.88 = f32[3,2,16,64,256]{4,3,0,1,2:T(8,128)} copy(f32[3,2,16,64,256]{4,2,3,0,1:T(8,128)S(1)} %pad_maximum_fusion) | data formatting | bytes 12582912 | tf_op jit(solution)/shard_map/stack | solution.py:109
  61.3 4.9 all-to-all-start.2
  66.4 71.3 %all-to-all-done.2 = f32[3,2,16,64,256]{4,3,0,1,2:T(8,128)} async-done(((f32[3,2,16,64,256]{4,3,0,1,2:T(8,128)}), f32[3,2,16,64,256]{4,3,0,1,2:T(8,128)}, u32[]{:S(2)}, u32[]{:S(2)}) %all-to-all-start.2) | async-done | bytes 6291488 | tf_op jit(solution)/shard_map/all_to_all | solution.py:112
  137.7 3.5 copy.90
  141.2 0.4 fusion.246
  141.6 4.8 fusion.38
  146.4 4.8 fusion.36
  151.3 5.3 multiply_subtract_fusion.3
  156.5 5.7 multiply_subtract_fusion.2
  162.2 5.5 fusion.30
  167.7 5.0 fusion.28
  172.7 5.4 multiply_subtract_fusion.1
  178.1 1.8 copy.97
  179.9 5.3 multiply_add_fusion.1
  185.2 1.8 copy.100
  187.4 7.7 %copy.101 = f32[3,2,2,512,256]{4,2,0,1,3:T(2,128)} copy(f32[3,2,2,512,256]{4,3,2,0,1:T(8,128)S(1)} %pad_maximum_fusion.1) | data formatting | bytes 12582912 | tf_op jit(solution)/shard_map/stack | solution.py:114
  195.2 75.2 %all_to_all.87 = f32[3,2,2,512,256]{4,2,0,1,3:T(2,128)S(1)} all-to-all(f32[3,2,2,512,256]{4,2,0,1,3:T(2,128)} %copy.101), channel_id=1, replica_groups=mesh['seq'=8,'chan'=4] {'seq'}, dimensions={3} | all-to-all | bytes 12582912 | tf_op jit(solution)/shard_map/all_to_all | solution.py:115
  270.4 1.2 copy.102
  271.6 0.8 copy.103
  272.4 0.7 subtract_bitcast_fusion.2
  274.0 0.8 pad_maximum_fusion.2
  274.8 3.4 copy.104
  278.1 4.7 all-to-all-start.4
  282.9 0.4 all-reduce.2.cloned.1.call-start
  283.4 71.1 %all-to-all-done.4 = f32[3,2,16,64,256]{4,3,1,0,2:T(8,128)} async-done(((f32[3,2,16,64,256]{4,3,1,0,2:T(8,128)}), f32[3,2,16,64,256]{4,3,1,0,2:T(8,128)}, u32[]{:S(2)}, u32[]{:S(2)}) %all-to-all-start.4) | async-done | bytes 6291488 | tf_op jit(solution)/shard_map/all_to_all | solution.py:116
  354.5 3.5 copy.106
  358.4 4.8 fusion.22
  363.2 4.8 fusion.20
  368.1 5.0 fusion.44
  373.1 5.6 multiply_subtract_fusion
  378.8 5.3 fusion.14
  384.0 5.0 fusion.12
  389.1 5.1 fusion.50
  394.1 2.3 copy.113
  396.4 5.1 fusion.53
  401.5 1.8 copy.116
  403.3 0.4 pad_maximum_fusion.3
  403.7 7.7 %copy.117 = f32[3,2,2,512,256]{4,2,0,1,3:T(2,128)} copy(f32[3,2,2,512,256]{4,3,2,0,1:T(8,128)S(1)} %pad_maximum_fusion.3) | data formatting | bytes 12582912 | tf_op jit(solution)/shard_map/stack | solution.py:120
  411.4 75.2 %all_to_all.88 = f32[3,2,2,512,256]{4,2,0,1,3:T(2,128)S(1)} all-to-all(f32[3,2,2,512,256]{4,2,0,1,3:T(2,128)} %copy.117), channel_id=1, replica_groups=mesh['seq'=8,'chan'=4] {'seq'}, dimensions={3} | all-to-all | bytes 12582912 | tf_op jit(solution)/shard_map/all_to_all | solution.py:122
  486.7 1.2 copy.118
  487.9 7.5 %copy.119 = f32[3,2,8,2,64,256]{5,3,2,4,0,1:T(2,128)} copy(f32[3,2,8,2,64,256]{5,4,2,3,1,0:T(8,128)S(1)} %bitcast.228) | data formatting | bytes 12582912 | tf_op jit(solution)/shard_map/all_to_all | solution.py:122
  495.4 8.5 %all_to_all.78 = f32[3,2,16,64,256]{4,2,3,0,1:T(8,128)} reshape(f32[3,2,8,2,64,256]{5,3,2,4,0,1:T(2,128)} %copy.119) | data formatting | bytes 12582912 | tf_op jit(solution)/shard_map/all_to_all | solution.py:122
  503.9 4.3 fusion.4
  508.2 4.4 multiply_bitcast_fusion
  512.6 0.5 copy.120
  513.2 23.5 %all_to_all.89 = f32[3,8,64,256]{3,2,0,1:T(8,128)S(1)} all-to-all(f32[3,8,64,256]{3,2,0,1:T(8,128)S(1)} %copy.120), channel_id=1, replica_groups=mesh['seq'=8,'chan'=4] {'seq'}, dimensions={1} | all-to-all | bytes 3145728 | tf_op jit(solution)/shard_map/all_to_all | solution.py:131
  536.7 0.9 fusion.247
  537.7 1.2 multiply_reduce_fusion
  538.9 12.8 %psum.14 = f32[256]{0:T(256)} all-reduce(f32[256]{0:T(256)S(1)} %get-tuple-element.26), channel_id=1, replica_groups=mesh['seq'=8,'chan'=4] {'seq'}, use_global_device_ids=true, to_apply=%region_1.2 | all-reduce | flops 256 | bytes 2048 | tf_op jit(solution)/shard_map/psum | solution.py:141
  551.7 23.8 %all-reduce.2.cloned.1.call-done = f32[512,256]{1,0:T(8,128)} async-done(((f32[512,256]{1,0:T(8,128)}), f32[512,256]{1,0:T(8,128)}) %all-reduce.2.cloned.1.call-update) | async-done | bytes 524304 | tf_op jit(solution)/shard_map/psum | solution.py:135
  575.5 1.9 copy.193
  (25 shorter events, 2.2 us)
Async XLA Ops:
  9.4 0.7 copy-start
  11.3 20.6 %all-to-all-start = ((f32[2,8,64,256]{3,2,0,1:T(8,128)}), f32[2,8,64,256]{3,2,0,1:T(8,128)S(1)}, u32[]{:S(2)}, u32[]{:S(2)}) async-start(f32[2,8,64,256]{3,2,0,1:T(8,128)} %copy.84), calls=%async_computation | async-start | bytes 2097152 | tf_op jit(solution)/shard_map/all_to_all | solution.py:93
  31.9 13.9 %all-to-all-start.1 = ((f32[1,8,64,256]{3,2,0,1:T(8,128)}), f32[1,8,64,256]{3,2,0,1:T(8,128)}, u32[]{:S(2)}, u32[]{:S(2)}) async-start(f32[1,8,64,256]{3,2,0,1:T(8,128)} %bitcast.9), calls=%async_computation.1 | async-start | bytes 1048576 | tf_op jit(solution)/shard_map/all_to_all | solution.py:94
  61.3 76.4 %all-to-all-start.2 = ((f32[3,2,16,64,256]{4,3,0,1,2:T(8,128)}), f32[3,2,16,64,256]{4,3,0,1,2:T(8,128)}, u32[]{:S(2)}, u32[]{:S(2)}) async-start(f32[3,2,16,64,256]{4,3,0,1,2:T(8,128)} %copy.88), calls=%async_computation.2 | async-start | bytes 12582912 | tf_op jit(solution)/shard_map/all_to_all | solution.py:112
  278.1 76.4 %all-to-all-start.4 = ((f32[3,2,16,64,256]{4,3,1,0,2:T(8,128)}), f32[3,2,16,64,256]{4,3,1,0,2:T(8,128)}, u32[]{:S(2)}, u32[]{:S(2)}) async-start(f32[3,2,16,64,256]{4,3,1,0,2:T(8,128)} %copy.104), calls=%async_computation.4 | async-start | bytes 12582912 | tf_op jit(solution)/shard_map/all_to_all | solution.py:116
  282.9 292.6 %all-reduce.2.cloned.1.call-start = ((), (), s32[]{:S(2)}) async-start(), calls=%async_computation.7 | async-start | bytes 1048576 | tf_op jit(solution)/shard_map/psum | solution.py:135
  513.1 24.6 %copy-start.1 = (bf16[512,256]{1,0:T(8,128)(2,1)S(1)}, bf16[512,256]{1,0:T(8,128)(2,1)}, u32[]{:S(2)}) copy-start(bf16[512,256]{1,0:T(8,128)(2,1)} %copy-done) | copy-start | bytes 786436
  513.1 24.6 %copy-start.2 = (bf16[512,256]{1,0:T(8,128)(2,1)S(1)}, bf16[512,256]{1,0:T(8,128)(2,1)}, u32[]{:S(2)}) copy-start(bf16[512,256]{1,0:T(8,128)(2,1)} %param.9) | copy-start | bytes 786436
  513.1 24.6 %copy-start.3 = (bf16[512,256]{1,0:T(8,128)(2,1)S(1)}, bf16[512,256]{1,0:T(8,128)(2,1)}, u32[]{:S(2)}) copy-start(bf16[512,256]{1,0:T(8,128)(2,1)} %param.8) | copy-start | bytes 786436
  513.1 24.6 %copy-start.4 = (bf16[512,256]{1,0:T(8,128)(2,1)S(1)}, bf16[512,256]{1,0:T(8,128)(2,1)}, u32[]{:S(2)}) copy-start(bf16[512,256]{1,0:T(8,128)(2,1)} %param.6) | copy-start | bytes 786436
  513.2 24.6 %copy-start.5 = (f32[256]{0:T(256)S(1)}, f32[256]{0:T(256)}, u32[]{:S(2)}) copy-start(f32[256]{0:T(256)} %param.10) | copy-start | bytes 3076
Sparse Core Ops, SparseCore 0:
  537.8 37.6 all-reduce.1
where the time goes:
time: 594 us; the launch traced here: 584 us
  waiting for transfers between devices  191 us (32%)
  blocking collectives  187 us (31%)
  matrix products  97.7 us (16%)
  local copies, waits for them, and re-layouts  66.9 us (11%)
  starting transfers between devices  19.4 us (3%)
  between operations  14.7 us (2%)
  other arithmetic  8.38 us (1%)
    all_to_all x1, blocking collectives, body(): lax.all_to_all(back_cols, 'seq', split_axis=3, concat_axis=2, tiled=True)  75.2 us
    all_to_all x1, blocking collectives, body(): lax.all_to_all(spectra, 'seq', split_axis=3, concat_axis=2, tiled=True)  75.2 us
    all_to_all x1, waiting for transfers between devices, body(): lax.all_to_all(twisted, 'seq', split_axis=2, concat_axis=3, tiled=True)  71.3 us
    all_to_all x1, waiting for transfers between devices, body(): lax.all_to_all(spectral_products(blocks), 'seq', split_axis=2, concat_axi...  71.1 us
    psum x1, waiting for transfers between devices, body(): taps_grad = lax.psum(filt_grad, 'chan')  23.8 us
    all_to_all x1, blocking collectives, body(): lax.all_to_all(results, 'seq', split_axis=1, concat_axis=1, tiled=True)  23.5 us
    all_to_all x3, local copies, waits for them, and re-layouts, body(): lax.all_to_all(back_cols, 'seq', split_axis=3, concat_axis=2, tiled=True)  17.2 us
    all_to_all x1, waiting for transfers between devices, body(): lax.all_to_all(pair_rows, 'seq', split_axis=1, concat_axis=1, tiled=True)  15.4 us
  transfers between devices with their start and end apart: 5, of which 5 were waited for; matrix products, arithmetic and copies ran while one was open for 0% of the time, Pallas kernels for 0%

commit v1 on v0

v1 whole, which is shorter than its diff:
```python
import functools
import math

import jax
import jax.numpy as jnp
import numpy as np
from jax import lax
from jax.experimental import pallas as pl
from jax.experimental.pallas import tpu as pltpu
from jax.sharding import PartitionSpec as P

INNER = 256


def scaled(x, factor):
    if x is None or factor == 0.0:
        return None
    if factor == 1.0:
        return x
    if factor == -1.0:
        return -x
    return x * factor


def plus(a, b):
    if a is None:
        return b
    if b is None:
        return a
    return a + b


def minus(a, b):
    if b is None:
        return a
    if a is None:
        return -b
    return a - b


def turn(z, index, count, sign):
    re, im = z
    quarter = {0: (1.0, 0.0), 1: (0.0, 1.0), 2: (-1.0, 0.0), 3: (0.0, -1.0)}
    if 4 * index % count == 0:
        cos_v, sin_v = quarter[4 * index // count % 4]
    else:
        cos_v = math.cos(2.0 * math.pi * index / count)
        sin_v = math.sin(2.0 * math.pi * index / count)
    sin_v *= sign
    return (
        minus(scaled(re, cos_v), scaled(im, sin_v)),
        plus(scaled(im, cos_v), scaled(re, sin_v)),
    )


def small_rfft(rows):
    count = len(rows)
    if count == 1:
        return [(rows[0], None)]
    even = small_rfft(rows[0::2])
    odd = small_rfft(rows[1::2])
    out = [None] * (count // 2 + 1)
    for k in range(count // 4 + 1):
        t = turn(odd[k], k, count, -1.0)
        e = even[k]
        out[k] = (plus(e[0], t[0]), plus(e[1], t[1]))
        if count // 2 - k != k:
            out[count // 2 - k] = (minus(e[0], t[0]), minus(t[1], e[1]))
    return out


def small_irfft(spec, count):
    if count == 1:
        return [spec[0][0]]
    half = count // 2
    even, odd = [], []
    for k in range(count // 4 + 1):
        a, b = spec[k], spec[half - k]
        even.append((plus(a[0], b[0]), minus(a[1], b[1])))
        odd.append(turn((minus(a[0], b[0]), plus(a[1], b[1])), k, count, 1.0))
    if half == 1:
        even = [(spec[0][0] + spec[1][0], None)]
        odd = [(spec[0][0] - spec[1][0], None)]
    out = [None] * count
    out[0::2] = small_irfft(even, half)
    out[1::2] = small_irfft(odd, half)
    return out


def tables(outer):
    length = outer * INNER
    j = np.arange(INNER)
    k = np.arange(outer // 2 + 1)
    inner = 2.0 * np.pi * (np.outer(j, j) % INNER) / INNER
    c, s = np.cos(inner), np.sin(inner)
    forward = np.block([[c, -s], [s, c]])
    backward = np.block([[c, s], [-s, c]])
    twist = 2.0 * np.pi * (np.outer(k, j) % length) / length
    return forward, backward, np.cos(twist), np.sin(twist)


MESH = pl.DeviceIdType.MESH
MIXED, GATED, TAPS, CONV, CORR, FSUM, SKIP = range(7)


def split(x):
    high = x.astype(jnp.bfloat16)
    return high, (x - high.astype(jnp.float32)).astype(jnp.bfloat16)


def kernel(
    shards, groups, gate_in, out_gate, value_in, out_grad, skip_gain, taps, fwd_hi, fwd_lo,
    bwd_hi, bwd_lo, cos_t, sin_t, grad_gate, grad_out_gate, grad_value, skip_grad, taps_grad,
    sbuf, rbuf, a_hi, a_lo, spec, wide, obuf, nbuf, fbuf, zbuf, fsum, frecv, tbuf, kbuf, krecv,
    send_sem, recv_sem, zsend_sem, zrecv_sem,
):
    f32 = jnp.float32
    rows, channels = gate_in.shape
    own = channels // shards
    width = own // groups
    pieces = rows // INNER
    blocks = shards * pieces
    outer = 2 * blocks
    half = outer // 2 + 1
    length = outer * INNER
    me = lax.axis_index("seq")
    zme = lax.axis_index("chan")

    def peer(d):
        return lax.rem(me + d, shards)

    def zpeer(d):
        return lax.rem(zme + d, groups)

    def each(count, fn):
        def step(d, carry):
            fn(d)
            return carry

        lax.fori_loop(1, count, step, 0)

    def copy(slot, src, dst, to, source):
        return pltpu.make_async_remote_copy(
            src_ref=src, dst_ref=dst, send_sem=send_sem.at[slot, to],
            recv_sem=recv_sem.at[slot, source], device_id={"seq": to}, device_id_type=MESH,
        )

    def zcopy(slot, src, dst, to, source):
        return pltpu.make_async_remote_copy(
            src_ref=src, dst_ref=dst, send_sem=zsend_sem.at[slot, to],
            recv_sem=zrecv_sem.at[slot, source], device_id={"chan": to}, device_id_type=MESH,
        )

    places = {
        MIXED: (lambda p: sbuf.at[0, p], lambda q: rbuf.at[0, q]),
        GATED: (lambda p: sbuf.at[1, p], lambda q: rbuf.at[1, q]),
        TAPS: (lambda p: sbuf.at[2, p], lambda q: rbuf.at[2, q]),
        CONV: (lambda p: obuf.at[0, p], lambda q: nbuf.at[0, q]),
        CORR: (lambda p: obuf.at[1, p], lambda q: nbuf.at[1, q]),
        FSUM: (lambda p: fsum.at[p], lambda q: frecv.at[q]),
        SKIP: (lambda p: kbuf, lambda q: krecv.at[q]),
    }
    zplaces = [
        (lambda p: fbuf.at[p], lambda q: zbuf.at[q]),
        (lambda p: frecv, lambda q: tbuf.at[q]),
    ]

    def send(slot):
        src, dst = places[slot]
        each(shards, lambda d: copy(slot, src(peer(d)), dst(me), peer(d), me).start())

    def arrive(slot):
        dst = places[slot][1]
        each(
            shards,
            lambda d: copy(slot, dst(peer(d)), dst(peer(d)), peer(d), peer(d)).wait_recv(),
        )

    def sent(slot):
        src, dst = places[slot]
        each(shards, lambda d: copy(slot, src(peer(d)), dst(me), peer(d), me).wait_send())

    def zsend(slot):
        src, dst = zplaces[slot]
        each(groups, lambda d: zcopy(slot, src(zpeer(d)), dst(zme), zpeer(d), zme).start())

    def zarrive(slot):
        dst = zplaces[slot][1]
        each(
            groups,
            lambda d: zcopy(slot, dst(zpeer(d)), dst(zpeer(d)), zpeer(d), zpeer(d)).wait_recv(),
        )

    def zsent(slot):
        src, dst = zplaces[slot]
        each(groups, lambda d: zcopy(slot, src(zpeer(d)), dst(zme), zpeer(d), zme).wait_send())

    barrier = pltpu.get_barrier_semaphore()
    each(
        shards,
        lambda d: pl.semaphore_signal(
            barrier, inc=1, device_id={"seq": peer(d)}, device_id_type=MESH
        ),
    )
    each(
        groups,
        lambda d: pl.semaphore_signal(
            barrier, inc=1, device_id={"chan": zpeer(d)}, device_id_type=MESH
        ),
    )

    def product(a, b, at):
        x = a[:, at : at + 128].astype(f32) * b[:, at : at + 128].astype(f32)
        return x.astype(jnp.bfloat16).astype(f32)

    per = 128 // own

    def put(field, at, value):
        sbuf[field, at // own : at // own + per] = value.T.reshape(per, own, rows)

    def keep(field):
        rbuf[field, me] = sbuf[field, me]

    for at in range(0, channels, 128):
        put(0, at, product(gate_in, value_in, at))
    pl.semaphore_wait(barrier, shards - 1 + groups - 1)
    send(MIXED)
    for at in range(0, channels, 128):
        put(1, at, product(out_grad, out_gate, at))
    send(GATED)
    for at in range(0, channels, 128):
        put(2, at, taps[:, at : at + 128])
    send(TAPS)
    for at in range(0, channels, 128):
        both = product(gate_in, value_in, at) * product(out_grad, out_gate, at)
        kbuf[:, at : at + 128] = jnp.sum(both.reshape(rows // 8, 8, 128), axis=0)
    send(SKIP)
    krecv[me] = kbuf[...]
    for field in range(3):
        keep(field)

    def forward(field):
        def tile(g, carry):
            at = pl.ds(pl.multiple_of(g * 16, 16), 16)
            for lane in range(0, INNER, 128):
                series = []
                for i in range(blocks):
                    low = (i % pieces) * INNER + lane
                    series.append(rbuf[field, i // pieces, at, low : low + 128])
                for k, (re, im) in enumerate(small_rfft(series + [None] * blocks)):
                    c = cos_t[k : k + 1, lane : lane + 128]
                    s = sin_t[k : k + 1, lane : lane + 128]
                    tr = re * c if im is None else re * c + im * s
                    ti = -(re * s) if im is None else im * c - re * s
                    for z, low in ((tr, lane), (ti, INNER + lane)):
                        high, rest = split(z)
                        a_hi[k, at, low : low + 128] = high
                        a_lo[k, at, low : low + 128] = rest
            return carry

        lax.fori_loop(0, own // 16, tile, 0)
        spec[field] = times(fwd_hi, fwd_lo)

    def times(hi, lo):
        ah = a_hi[...].reshape(half * own, 2 * INNER)
        al = a_lo[...].reshape(half * own, 2 * INNER)
        out = jnp.dot(ah, hi[...], preferred_element_type=f32)
        out += jnp.dot(al, hi[...], preferred_element_type=f32)
        out += jnp.dot(ah, lo[...], preferred_element_type=f32)
        return out.reshape(half, own, 2 * INNER)

    def backward(first, second, conjugate, store):
        def multiply(k, carry):
            ar, ai = spec[first, k, :, :INNER], spec[first, k, :, INNER:]
            br, bi = spec[second, k, :, :INNER], spec[second, k, :, INNER:]
            if conjugate:
                re, im = ar * br + ai * bi, ai * br - ar * bi
            else:
                re, im = ar * br - ai * bi, ar * bi + ai * br
            high, rest = split(re)
            a_hi[k, :, :INNER] = high
            a_lo[k, :, :INNER] = rest
            high, rest = split(im)
            a_hi[k, :, INNER:] = high
            a_lo[k, :, INNER:] = rest
            return carry

        lax.fori_loop(0, half, multiply, 0)
        wide[...] = times(bwd_hi, bwd_lo)

        def tile(g, carry):
            at = pl.ds(pl.multiple_of(g * 8, 8), 8)
            for lane in range(0, INNER, 128):
                items = []
                for k in range(half):
                    br = wide[k, at, lane : lane + 128]
                    bi = wide[k, at, INNER + lane : INNER + lane + 128]
                    c = cos_t[k : k + 1, lane : lane + 128] * (1.0 / length)
                    s = sin_t[k : k + 1, lane : lane + 128] * (1.0 / length)
                    items.append((br * c - bi * s, bi * c + br * s))
                out = small_irfft(items, outer)
                for i in range(blocks):
                    store(g, i // pieces, (i % pieces) * INNER + lane, out[i])
            return carry

        lax.fori_loop(0, own // 8, tile, 0)

    def store_in(field):
        def store(g, block, low, value):
            at = pl.ds(pl.multiple_of(g * 8, 8), 8)
            obuf[field, block, at, low : low + 128] = value

        return store

    def store_filter(g, block, low, value):
        for u in range(8 // width):
            part = value[u * width : (u + 1) * width]
            fbuf[g * (8 // width) + u, block, :, low : low + 128] = part

    arrive(MIXED)
    forward(0)
    arrive(GATED)
    forward(1)
    backward(1, 0, True, store_filter)
    zsend(0)
    zbuf[zme] = fbuf[zme]
    arrive(TAPS)
    forward(2)
    backward(2, 0, False, store_in(0))
    send(CONV)
    nbuf[0, me] = obuf[0, me]
    zarrive(0)
    total = zbuf[0]
    for z in range(1, groups):
        total = total + zbuf[z]
    fsum[...] = total
    send(FSUM)
    frecv[me] = fsum[me]
    backward(1, 2, True, store_in(1))
    send(CORR)
    nbuf[1, me] = obuf[1, me]
    arrive(FSUM)
    zsend(1)
    tbuf[zme] = frecv[...]
    arrive(SKIP)
    skips = krecv[0]
    for q in range(1, shards):
        skips = skips + krecv[q]
    skip_grad[...] = jnp.sum(skips, axis=0, keepdims=True)

    def natural(field, at):
        first = at // own
        return nbuf[field, first : first + per].reshape(128, rows).T

    arrive(CONV)
    for at in range(0, channels, 128):
        cols = slice(at, at + 128)
        mixed = product(gate_in, value_in, at)
        inner = natural(0, at) + skip_gain[:, cols] * mixed
        grad_out_gate[:, cols] = (out_grad[:, cols].astype(f32) * inner).astype(jnp.bfloat16)
    arrive(CORR)
    for at in range(0, channels, 128):
        cols = slice(at, at + 128)
        mix_grad = natural(1, at) + skip_gain[:, cols] * product(out_grad, out_gate, at)
        grad_gate[:, cols] = (mix_grad * value_in[:, cols].astype(f32)).astype(jnp.bfloat16)
        grad_value[:, cols] = (mix_grad * gate_in[:, cols].astype(f32)).astype(jnp.bfloat16)
    zarrive(1)
    for at in range(0, channels, 128):
        parts = [
            tbuf[z, q]
            for q in range(at // own, at // own + per)
            for z in range(groups)
        ]
        taps_grad[:, at : at + 128] = jnp.concatenate(parts, axis=0).T
    for slot in range(7):
        sent(slot)
    for slot in range(2):
        zsent(slot)


def body(gate_in, out_gate, value_in, out_grad, skip_gain, filter_taps):
    f32, bf16 = jnp.float32, jnp.bfloat16
    shards = lax.axis_size("seq")
    groups = lax.axis_size("chan")
    rows, channels = gate_in.shape
    own = channels // shards
    width = own // groups
    outer = 2 * shards * (rows // INNER)
    half = outer // 2 + 1
    forward, backward, cos_t, sin_t = tables(outer)
    mats = []
    for m in (forward, backward):
        high = m.astype(bf16)
        mats += [jnp.asarray(high), jnp.asarray((m - high.astype(np.float64)).astype(bf16))]
    vmem = pl.BlockSpec(memory_space=pltpu.VMEM)
    outs = pl.pallas_call(
        functools.partial(kernel, shards, groups),
        out_shape=(
            jax.ShapeDtypeStruct((rows, channels), bf16),
            jax.ShapeDtypeStruct((rows, channels), bf16),
            jax.ShapeDtypeStruct((rows, channels), bf16),
            jax.ShapeDtypeStruct((1, channels), f32),
            jax.ShapeDtypeStruct((rows, channels), f32),
        ),
        in_specs=[vmem] * 12,
        out_specs=(vmem,) * 5,
        scratch_shapes=[
            pltpu.VMEM((3, shards, own, rows), f32),
            pltpu.VMEM((3, shards, own, rows), f32),
            pltpu.VMEM((half, own, 2 * INNER), bf16),
            pltpu.VMEM((half, own, 2 * INNER), bf16),
            pltpu.VMEM((3, half, own, 2 * INNER), f32),
            pltpu.VMEM((half, own, 2 * INNER), f32),
            pltpu.VMEM((2, shards, own, rows), f32),
            pltpu.VMEM((2, shards, own, rows), f32),
            pltpu.VMEM((groups, shards, width, rows), f32),
            pltpu.VMEM((groups, shards, width, rows), f32),
            pltpu.VMEM((shards, width, rows), f32),
            pltpu.VMEM((shards, width, rows), f32),
            pltpu.VMEM((groups, shards, width, rows), f32),
            pltpu.VMEM((8, channels), f32),
            pltpu.VMEM((shards, 8, channels), f32),
            pltpu.SemaphoreType.DMA((7, shards)),
            pltpu.SemaphoreType.DMA((7, shards)),
            pltpu.SemaphoreType.DMA((2, groups)),
            pltpu.SemaphoreType.DMA((2, groups)),
        ],
        compiler_params=pltpu.CompilerParams(
            collective_id=0, has_side_effects=True, vmem_limit_bytes=50 * 2**20
        ),
        name="hyena",
    )(
        gate_in, out_gate, value_in, out_grad, skip_gain.reshape(1, channels), filter_taps,
        *mats, jnp.asarray(cos_t, f32), jnp.asarray(sin_t, f32),
    )
    return (outs[0], outs[1], outs[2], outs[3].reshape(channels), outs[4])


def solution(mesh):
    wide = P("seq", "chan")
    return jax.shard_map(
        body,
        mesh=mesh,
        in_specs=(wide, wide, wide, wide, P("chan"), P("seq", None)),
        out_specs=(wide, wide, wide, P("chan"), P("seq", None)),
        check_vma=False,
    )
```

time: 594 us -> 65.4 us (0.11)
  the two profiles are of different devices: /device:TPU:0 before, /device:TPU:24 now
where the time goes in v1:
time: 65.4 us; the launch traced here: 64.9 us
  Pallas kernels  51.7 us (79%)
  local copies, waits for them, and re-layouts  12.5 us (19%)
  between operations  0.66 us (1%)
    pallas_call x1, Pallas kernels, body(): pl.pallas_call(functools.partial(kernel, shards, groups), out_shape=(jax....  51.7 us
    unnamed x25, local copies, waits for them, and re-layouts  12.5 us

profile of v1, /device:TPU:24, one launch (start us, length us, event | category | flops | bytes accessed | tf_op | source)
XLA Modules:
  0.0 64.9 jit_solution(14896950176836527003)
XLA Ops:
  0.6 0.0 copy-start.9
  0.6 0.7 %copy-done.9 = f32[256]{0:T(256)S(1)} copy-done((f32[256]{0:T(256)S(1)}, f32[256]{0:T(256)}, u32[]{:S(2)}) %copy-start.9) | copy-done | bytes 1048
  1.3 0.0 copy-start
  1.3 1.0 %copy-done = f32[512,256]{1,0:T(8,128)S(1)} copy-done((f32[512,256]{1,0:T(8,128)S(1)}, f32[512,256]{1,0:T(8,128)}, u32[]{:S(2)}) %copy-start) | copy-done | bytes 524312
  2.4 0.0 copy-start.1
  2.4 1.0 %copy-done.1 = bf16[512,512]{1,0:T(8,128)(2,1)S(1)} copy-done((bf16[512,512]{1,0:T(8,128)(2,1)S(1)}, bf16[512,512]{1,0:T(8,128)(2,1)}, u32[]{:S(2)}) %copy-start.1) | copy-done | bytes 524312
  3.4 0.0 copy-start.2
  3.4 1.0 %copy-done.2 = bf16[512,512]{1,0:T(8,128)(2,1)S(1)} copy-done((bf16[512,512]{1,0:T(8,128)(2,1)S(1)}, bf16[512,512]{1,0:T(8,128)(2,1)}, u32[]{:S(2)}) %copy-start.2) | copy-done | bytes 524312
  4.4 0.0 copy-start.3
  4.4 0.9 %copy-done.3 = bf16[512,256]{1,0:T(8,128)(2,1)S(1)} copy-done((bf16[512,256]{1,0:T(8,128)(2,1)S(1)}, bf16[512,256]{1,0:T(8,128)(2,1)}, u32[]{:S(2)}) %copy-start.3) | copy-done | bytes 262168
  5.4 0.0 copy-start.4
  5.4 0.9 %copy-done.4 = bf16[512,256]{1,0:T(8,128)(2,1)S(1)} copy-done((bf16[512,256]{1,0:T(8,128)(2,1)S(1)}, bf16[512,256]{1,0:T(8,128)(2,1)}, u32[]{:S(2)}) %copy-start.4) | copy-done | bytes 262168
  6.3 0.0 copy-start.5
  6.3 0.9 %copy-done.5 = bf16[512,256]{1,0:T(8,128)(2,1)S(1)} copy-done((bf16[512,256]{1,0:T(8,128)(2,1)S(1)}, bf16[512,256]{1,0:T(8,128)(2,1)}, u32[]{:S(2)}) %copy-start.5) | copy-done | bytes 262168
  7.3 0.0 copy-start.6
  7.3 0.9 %copy-done.6 = bf16[512,256]{1,0:T(8,128)(2,1)S(1)} copy-done((bf16[512,256]{1,0:T(8,128)(2,1)S(1)}, bf16[512,256]{1,0:T(8,128)(2,1)}, u32[]{:S(2)}) %copy-start.6) | copy-done | bytes 262168
  8.2 0.0 copy-start.7
  8.2 0.7 %copy-done.7 = f32[17,256]{1,0:T(8,128)S(1)} copy-done((f32[17,256]{1,0:T(8,128)S(1)}, f32[17,256]{1,0:T(8,128)}, u32[]{:S(2)}) %copy-start.7) | copy-done | bytes 17432
  9.0 0.0 copy-start.8
  9.0 0.7 %copy-done.8 = f32[17,256]{1,0:T(8,128)S(1)} copy-done((f32[17,256]{1,0:T(8,128)S(1)}, f32[17,256]{1,0:T(8,128)}, u32[]{:S(2)}) %copy-start.8) | copy-done | bytes 17432
  9.7 51.7 %hyena.1 = (bf16[512,256]{1,0:T(8,128)(2,1)S(1)}, bf16[512,256]{1,0:T(8,128)(2,1)S(1)}, bf16[512,256]{1,0:T(8,128)(2,1)S(1)}, f32[1,256]{1,0:T(1,128)S(1)}, f32[512,256]{1,0:T(8,128)S(1)}) custom-call(bf16[512,256]{1,0:T(8,128)(2,1)S(1)} %copy-done.3, bf16[512,256]{1,0:T(8,128)(2,1)S(1)} %copy-done.4, bf16[512,256]{1,0:T(8,128)(2,1)S(1)} %copy-done.5, ...), custom_call_target="tpu_custom_call" | custom-call | tf_op jit(solution)/shard_map/hyena/pallas_call | solution.py:396
  61.4 0.7 %copy.22 = bf16[512,256]{1,0:T(8,128)(2,1)} copy(bf16[512,256]{1,0:T(8,128)(2,1)S(1)} %get-tuple-element.20) | data formatting | bytes 524288
  62.1 0.7 %copy.23 = bf16[512,256]{1,0:T(8,128)(2,1)} copy(bf16[512,256]{1,0:T(8,128)(2,1)S(1)} %get-tuple-element.21) | data formatting | bytes 524288
  62.8 0.7 %copy.24 = bf16[512,256]{1,0:T(8,128)(2,1)} copy(bf16[512,256]{1,0:T(8,128)(2,1)S(1)} %get-tuple-element.22) | data formatting | bytes 524288
  63.5 0.6 copy.25
  64.1 0.8 %copy.26 = f32[512,256]{1,0:T(8,128)} copy(f32[512,256]{1,0:T(8,128)S(1)} %get-tuple-element.24) | data formatting | bytes 1048576
Async XLA Ops:
  0.6 0.7 %copy-start.9 = (f32[256]{0:T(256)S(1)}, f32[256]{0:T(256)}, u32[]{:S(2)}) copy-start(f32[256]{0:T(256)} %param.16) | copy-start | bytes 3076
  1.3 1.0 %copy-start = (f32[512,256]{1,0:T(8,128)S(1)}, f32[512,256]{1,0:T(8,128)}, u32[]{:S(2)}) copy-start(f32[512,256]{1,0:T(8,128)} %taps.1) | copy-start | bytes 1572868
  2.4 1.0 %copy-start.1 = (bf16[512,512]{1,0:T(8,128)(2,1)S(1)}, bf16[512,512]{1,0:T(8,128)(2,1)}, u32[]{:S(2)}) copy-start(bf16[512,512]{1,0:T(8,128)(2,1)} %constant.13.clone.fwd_lo) | copy-start | bytes 1572868
  3.4 1.0 %copy-start.2 = (bf16[512,512]{1,0:T(8,128)(2,1)S(1)}, bf16[512,512]{1,0:T(8,128)(2,1)}, u32[]{:S(2)}) copy-start(bf16[512,512]{1,0:T(8,128)(2,1)} %constant.12.clone.fwd_hi) | copy-start | bytes 1572868
  4.4 0.9 %copy-start.3 = (bf16[512,256]{1,0:T(8,128)(2,1)S(1)}, bf16[512,256]{1,0:T(8,128)(2,1)}, u32[]{:S(2)}) copy-start(bf16[512,256]{1,0:T(8,128)(2,1)} %gate_in.1) | copy-start | bytes 786436
  5.4 0.9 %copy-start.4 = (bf16[512,256]{1,0:T(8,128)(2,1)S(1)}, bf16[512,256]{1,0:T(8,128)(2,1)}, u32[]{:S(2)}) copy-start(bf16[512,256]{1,0:T(8,128)(2,1)} %out_gate.1) | copy-start | bytes 786436
  6.3 0.9 %copy-start.5 = (bf16[512,256]{1,0:T(8,128)(2,1)S(1)}, bf16[512,256]{1,0:T(8,128)(2,1)}, u32[]{:S(2)}) copy-start(bf16[512,256]{1,0:T(8,128)(2,1)} %value_in.1) | copy-start | bytes 786436
  7.3 0.9 %copy-start.6 = (bf16[512,256]{1,0:T(8,128)(2,1)S(1)}, bf16[512,256]{1,0:T(8,128)(2,1)}, u32[]{:S(2)}) copy-start(bf16[512,256]{1,0:T(8,128)(2,1)} %out_grad.1) | copy-start | bytes 786436
  8.2 0.7 %copy-start.7 = (f32[17,256]{1,0:T(8,128)S(1)}, f32[17,256]{1,0:T(8,128)}, u32[]{:S(2)}) copy-start(f32[17,256]{1,0:T(8,128)} %constant.17.clone.sin_t) | copy-start | bytes 52228
  9.0 0.7 %copy-start.8 = (f32[17,256]{1,0:T(8,128)S(1)}, f32[17,256]{1,0:T(8,128)}, u32[]{:S(2)}) copy-start(f32[17,256]{1,0:T(8,128)} %constant.16.clone.cos_t) | copy-start | bytes 52228

commit v2 on v1

--- a/solution.py
+++ b/solution.py
@@ -100,6 +100,7 @@
 
 
 MESH = pl.DeviceIdType.MESH
+LOAD_ORDER = (0, 2, 1, 3, 5, 10, 11, 6, 7, 8, 9, 4)
 MIXED, GATED, TAPS, CONV, CORR, FSUM, SKIP = range(7)
 
 
@@ -109,11 +110,23 @@
 
 
 def kernel(
-    shards, groups, gate_in, out_gate, value_in, out_grad, skip_gain, taps, fwd_hi, fwd_lo,
-    bwd_hi, bwd_lo, cos_t, sin_t, grad_gate, grad_out_gate, grad_value, skip_grad, taps_grad,
-    sbuf, rbuf, a_hi, a_lo, spec, wide, obuf, nbuf, fbuf, zbuf, fsum, frecv, tbuf, kbuf, krecv,
-    send_sem, recv_sem, zsend_sem, zrecv_sem,
+    shards, groups, *refs,
 ):
+    given, refs = refs[:12], refs[12:]
+    (
+        grad_gate, grad_out_gate, grad_value, skip_grad, taps_grad, load_sem, gate_in, out_gate,
+        value_in, out_grad, skip_gain, taps, fwd_hi, fwd_lo, bwd_hi, bwd_lo, cos_t, sin_t, sbuf, rbuf, a_hi, a_lo, spec, wide, obuf, nbuf, fbuf, zbuf, fsum, frecv, tbuf, kbuf, krecv,
+        send_sem, recv_sem, zsend_sem, zrecv_sem,
+    ) = refs
+    held = (
+        gate_in, out_gate, value_in, out_grad, skip_gain, taps, fwd_hi, fwd_lo, bwd_hi, bwd_lo,
+        cos_t, sin_t,
+    )
+    loads = [
+        pltpu.make_async_copy(given[i], held[i], load_sem.at[i]) for i in range(len(given))
+    ]
+    for i in LOAD_ORDER:
+        loads[i].start()
     f32 = jnp.float32
     rows, channels = gate_in.shape
     own = channels // shards
@@ -221,13 +234,18 @@
     def keep(field):
         rbuf[field, me] = sbuf[field, me]
 
+    loads[0].wait()
+    loads[2].wait()
     for at in range(0, channels, 128):
         put(0, at, product(gate_in, value_in, at))
     pl.semaphore_wait(barrier, shards - 1 + groups - 1)
     send(MIXED)
+    loads[1].wait()
+    loads[3].wait()
     for at in range(0, channels, 128):
         put(1, at, product(out_grad, out_gate, at))
     send(GATED)
+    loads[5].wait()
     for at in range(0, channels, 128):
         put(2, at, taps[:, at : at + 128])
     send(TAPS)
@@ -317,6 +335,8 @@
             part = value[u * width : (u + 1) * width]
             fbuf[g * (8 // width) + u, block, :, low : low + 128] = part
 
+    for i in (10, 11, 6, 7, 8, 9, 4):
+        loads[i].wait()
     arrive(MIXED)
     forward(0)
     arrive(GATED)
@@ -392,6 +412,10 @@
     for m in (forward, backward):
         high = m.astype(bf16)
         mats += [jnp.asarray(high), jnp.asarray((m - high.astype(np.float64)).astype(bf16))]
+    inputs = (
+        gate_in, out_gate, value_in, out_grad, skip_gain.reshape(1, channels), filter_taps,
+        *mats, jnp.asarray(cos_t, f32), jnp.asarray(sin_t, f32),
+    )
     vmem = pl.BlockSpec(memory_space=pltpu.VMEM)
     outs = pl.pallas_call(
         functools.partial(kernel, shards, groups),
@@ -402,9 +426,11 @@
             jax.ShapeDtypeStruct((1, channels), f32),
             jax.ShapeDtypeStruct((rows, channels), f32),
         ),
-        in_specs=[vmem] * 12,
+        in_specs=[pl.BlockSpec(memory_space=pltpu.HBM)] * 12,
         out_specs=(vmem,) * 5,
-        scratch_shapes=[
+        scratch_shapes=[pltpu.SemaphoreType.DMA((12,))]
+        + [pltpu.VMEM(x.shape, x.dtype) for x in inputs]
+        + [
             pltpu.VMEM((3, shards, own, rows), f32),
             pltpu.VMEM((3, shards, own, rows), f32),
             pltpu.VMEM((half, own, 2 * INNER), bf16),
@@ -426,13 +452,10 @@
             pltpu.SemaphoreType.DMA((2, groups)),
         ],
         compiler_params=pltpu.CompilerParams(
-            collective_id=0, has_side_effects=True, vmem_limit_bytes=50 * 2**20
+            collective_id=0, has_side_effects=True, vmem_limit_bytes=60 * 2**20
         ),
         name="hyena",
-    )(
-        gate_in, out_gate, value_in, out_grad, skip_gain.reshape(1, channels), filter_taps,
-        *mats, jnp.asarray(cos_t, f32), jnp.asarray(sin_t, f32),
-    )
+    )(*inputs)
     return (outs[0], outs[1], outs[2], outs[3].reshape(channels), outs[4])
 
 

time: 65.4 us -> 57.1 us (0.87)
  local copies, waits for them, and re-layouts: 12.5 us -> 4.5 us
    unnamed x25 -> x13, local copies, waits for them, and re-layouts: 12.5 us -> 4.5 us
where the time goes in v2:
time: 57.1 us; the launch traced here: 56.9 us
  Pallas kernels  51.8 us (91%)
  local copies, waits for them, and re-layouts  4.5 us (8%)
  between operations  0.66 us (1%)
    pallas_call x1, Pallas kernels, body(): pl.pallas_call(functools.partial(kernel, shards, groups), out_shape=(jax....  51.8 us
    unnamed x13, local copies, waits for them, and re-layouts  4.5 us

profile of v2, /device:TPU:24, one launch (start us, length us, event | category | flops | bytes accessed | tf_op | source)
XLA Modules:
  0.0 56.9 jit_solution(6557684837650137012)
XLA Ops:
  0.6 51.8 %hyena.1 = (bf16[512,256]{1,0:T(8,128)(2,1)}, bf16[512,256]{1,0:T(8,128)(2,1)}, bf16[512,256]{1,0:T(8,128)(2,1)}, f32[1,256]{1,0:T(1,128)}, f32[512,256]{1,0:T(8,128)}) custom-call(bf16[512,256]{1,0:T(8,128)(2,1)} %refs_0_.1, bf16[512,256]{1,0:T(8,128)(2,1)} %refs_1_.1, bf16[512,256]{1,0:T(8,128)(2,1)} %refs_2_.1, bf16[512,256]{1,0:T(8,128)(2,1)} %refs_3_.1, ...), custom_call_target="tpu_custom_call" | custom-call | tf_op jit(solution)/shard_map/hyena/pallas_call | solution.py:420
  52.4 0.0 copy-start.2
  52.4 0.0 copy-start.1
  52.4 1.7 %copy.22 = bf16[512,256]{1,0:T(8,128)(2,1)} copy(bf16[512,256]{1,0:T(8,128)(2,1)} %get-tuple-element.20) | data formatting | bytes 524288
  54.1 0.0 copy-done.2
  54.1 0.0 copy-start
  54.1 0.7 %copy.23 = bf16[512,256]{1,0:T(8,128)(2,1)} copy(bf16[512,256]{1,0:T(8,128)(2,1)S(1)} %copy-done.2) | data formatting | bytes 524288
  54.9 0.0 copy-done.1
  54.9 0.0 copy-start.3
  54.9 0.7 %copy.24 = bf16[512,256]{1,0:T(8,128)(2,1)} copy(bf16[512,256]{1,0:T(8,128)(2,1)S(1)} %copy-done.1) | data formatting | bytes 524288
  55.6 0.0 copy-done.3
  55.6 0.6 copy.25
  56.1 0.0 copy-done
  56.1 0.8 %copy.26 = f32[512,256]{1,0:T(8,128)} copy(f32[512,256]{1,0:T(8,128)S(1)} %copy-done) | data formatting | bytes 1048576
Async XLA Ops:
  52.4 1.7 %copy-start.2 = (bf16[512,256]{1,0:T(8,128)(2,1)S(1)}, bf16[512,256]{1,0:T(8,128)(2,1)}, u32[]{:S(2)}) copy-start(bf16[512,256]{1,0:T(8,128)(2,1)} %get-tuple-element.21) | copy-start | bytes 786436
  52.4 2.4 %copy-start.1 = (bf16[512,256]{1,0:T(8,128)(2,1)S(1)}, bf16[512,256]{1,0:T(8,128)(2,1)}, u32[]{:S(2)}) copy-start(bf16[512,256]{1,0:T(8,128)(2,1)} %get-tuple-element.22) | copy-start | bytes 786436
  54.1 2.0 %copy-start = (f32[512,256]{1,0:T(8,128)S(1)}, f32[512,256]{1,0:T(8,128)}, u32[]{:S(2)}) copy-start(f32[512,256]{1,0:T(8,128)} %get-tuple-element.24) | copy-start | bytes 1572868
  54.9 0.7 %copy-start.3 = (f32[1,256]{1,0:T(1,128)S(1)}, f32[1,256]{1,0:T(1,128)}, u32[]{:S(2)}) copy-start(f32[1,256]{1,0:T(1,128)} %get-tuple-element.13) | copy-start | bytes 3076

commit v3 on v2

--- a/solution.py
+++ b/solution.py
@@ -115,7 +115,7 @@
     given, refs = refs[:12], refs[12:]
     (
         grad_gate, grad_out_gate, grad_value, skip_grad, taps_grad, load_sem, gate_in, out_gate,
-        value_in, out_grad, skip_gain, taps, fwd_hi, fwd_lo, bwd_hi, bwd_lo, cos_t, sin_t, sbuf, rbuf, a_hi, a_lo, spec, wide, obuf, nbuf, fbuf, zbuf, fsum, frecv, tbuf, kbuf, krecv,
+        value_in, out_grad, skip_gain, taps, fwd_hi, fwd_lo, bwd_hi, bwd_lo, cos_t, sin_t, sbuf, rbuf, a_hi, a_lo, spec, wide, obuf, nbuf, fbuf, zbuf, fsum, frecv, tbuf, kbuf, krecv, tap_out, tap_in, tap_all,
         send_sem, recv_sem, zsend_sem, zrecv_sem,
     ) = refs
     held = (
@@ -167,7 +167,7 @@
     places = {
         MIXED: (lambda p: sbuf.at[0, p], lambda q: rbuf.at[0, q]),
         GATED: (lambda p: sbuf.at[1, p], lambda q: rbuf.at[1, q]),
-        TAPS: (lambda p: sbuf.at[2, p], lambda q: rbuf.at[2, q]),
+        TAPS: (lambda p: tap_out.at[zme, p], lambda q: tap_in.at[q]),
         CONV: (lambda p: obuf.at[0, p], lambda q: nbuf.at[0, q]),
         CORR: (lambda p: obuf.at[1, p], lambda q: nbuf.at[1, q]),
         FSUM: (lambda p: fsum.at[p], lambda q: frecv.at[q]),
@@ -176,6 +176,7 @@
     zplaces = [
         (lambda p: fbuf.at[p], lambda q: zbuf.at[q]),
         (lambda p: frecv, lambda q: tbuf.at[q]),
+        (lambda p: tap_in, lambda q: tap_all.at[q]),
     ]
 
     def send(slot):
@@ -240,22 +241,29 @@
         put(0, at, product(gate_in, value_in, at))
     pl.semaphore_wait(barrier, shards - 1 + groups - 1)
     send(MIXED)
+    loads[5].wait()
+    for at in range(0, channels, 128):
+        flipped = taps[:, at : at + 128].T
+        for u in range(128 // width):
+            row = at + u * width
+            tap_out[row % own // width, row // own] = flipped[u * width : (u + 1) * width]
+    send(TAPS)
+    tap_in[me] = tap_out[zme, me]
     loads[1].wait()
     loads[3].wait()
     for at in range(0, channels, 128):
         put(1, at, product(out_grad, out_gate, at))
     send(GATED)
-    loads[5].wait()
-    for at in range(0, channels, 128):
-        put(2, at, taps[:, at : at + 128])
-    send(TAPS)
     for at in range(0, channels, 128):
         both = product(gate_in, value_in, at) * product(out_grad, out_gate, at)
         kbuf[:, at : at + 128] = jnp.sum(both.reshape(rows // 8, 8, 128), axis=0)
     send(SKIP)
     krecv[me] = kbuf[...]
-    for field in range(3):
+    for field in range(2):
         keep(field)
+    arrive(TAPS)
+    zsend(2)
+    tap_all[zme] = tap_in[...]
 
     def forward(field):
         def tile(g, carry):
@@ -344,7 +352,9 @@
     backward(1, 0, True, store_filter)
     zsend(0)
     zbuf[zme] = fbuf[zme]
-    arrive(TAPS)
+    zarrive(2)
+    for z in range(groups):
+        rbuf[2, :, z * width : (z + 1) * width, :] = tap_all[z]
     forward(2)
     backward(2, 0, False, store_in(0))
     send(CONV)
@@ -394,7 +404,7 @@
         taps_grad[:, at : at + 128] = jnp.concatenate(parts, axis=0).T
     for slot in range(7):
         sent(slot)
-    for slot in range(2):
+    for slot in range(3):
         zsent(slot)
 
 
@@ -446,10 +456,13 @@
             pltpu.VMEM((groups, shards, width, rows), f32),
             pltpu.VMEM((8, channels), f32),
             pltpu.VMEM((shards, 8, channels), f32),
+            pltpu.VMEM((groups, shards, width, rows), f32),
+            pltpu.VMEM((shards, width, rows), f32),
+            pltpu.VMEM((groups, shards, width, rows), f32),
             pltpu.SemaphoreType.DMA((7, shards)),
             pltpu.SemaphoreType.DMA((7, shards)),
-            pltpu.SemaphoreType.DMA((2, groups)),
-            pltpu.SemaphoreType.DMA((2, groups)),
+            pltpu.SemaphoreType.DMA((3, groups)),
+            pltpu.SemaphoreType.DMA((3, groups)),
         ],
         compiler_params=pltpu.CompilerParams(
             collective_id=0, has_side_effects=True, vmem_limit_bytes=60 * 2**20

time: 57.1 us -> 63.2 us (1.11)
  Pallas kernels: 51.8 us -> 57.5 us
    pallas_call x1, Pallas kernels: 51.8 us -> 57.5 us  [body(): pl.pallas_call(functools.partial(kernel, shards, groups), out_shape=(jax....]
where the time goes in v3:
time: 63.2 us; the launch traced here: 62.7 us
  Pallas kernels  57.5 us (91%)
  local copies, waits for them, and re-layouts  4.5 us (7%)
  between operations  0.66 us (1%)
    pallas_call x1, Pallas kernels, body(): pl.pallas_call(functools.partial(kernel, shards, groups), out_shape=(jax....  57.5 us
    unnamed x13, local copies, waits for them, and re-layouts  4.5 us

profile of v3, /device:TPU:24, one launch (start us, length us, event | category | flops | bytes accessed | tf_op | source)
XLA Modules:
  0.0 62.7 jit_solution(9899456966884417262)
XLA Ops:
  0.6 57.5 %hyena.1 = (bf16[512,256]{1,0:T(8,128)(2,1)}, bf16[512,256]{1,0:T(8,128)(2,1)}, bf16[512,256]{1,0:T(8,128)(2,1)}, f32[1,256]{1,0:T(1,128)}, f32[512,256]{1,0:T(8,128)}) custom-call(bf16[512,256]{1,0:T(8,128)(2,1)} %refs_0_.1, bf16[512,256]{1,0:T(8,128)(2,1)} %refs_1_.1, bf16[512,256]{1,0:T(8,128)(2,1)} %refs_2_.1, bf16[512,256]{1,0:T(8,128)(2,1)} %refs_3_.1, ...), custom_call_target="tpu_custom_call" | custom-call | tf_op jit(solution)/shard_map/hyena/pallas_call | solution.py:430
  58.2 0.0 copy-start.2
  58.2 0.0 copy-start.1
  58.2 1.7 %copy.22 = bf16[512,256]{1,0:T(8,128)(2,1)} copy(bf16[512,256]{1,0:T(8,128)(2,1)} %get-tuple-element.20) | data formatting | bytes 524288
  59.9 0.0 copy-done.2
  59.9 0.0 copy-start
  59.9 0.7 %copy.23 = bf16[512,256]{1,0:T(8,128)(2,1)} copy(bf16[512,256]{1,0:T(8,128)(2,1)S(1)} %copy-done.2) | data formatting | bytes 524288
  60.6 0.0 copy-done.1
  60.6 0.0 copy-start.3
  60.6 0.7 %copy.24 = bf16[512,256]{1,0:T(8,128)(2,1)} copy(bf16[512,256]{1,0:T(8,128)(2,1)S(1)} %copy-done.1) | data formatting | bytes 524288
  61.3 0.0 copy-done.3
  61.3 0.6 copy.25
  61.9 0.0 copy-done
  61.9 0.8 %copy.26 = f32[512,256]{1,0:T(8,128)} copy(f32[512,256]{1,0:T(8,128)S(1)} %copy-done) | data formatting | bytes 1048576
Async XLA Ops:
  58.2 1.7 %copy-start.2 = (bf16[512,256]{1,0:T(8,128)(2,1)S(1)}, bf16[512,256]{1,0:T(8,128)(2,1)}, u32[]{:S(2)}) copy-start(bf16[512,256]{1,0:T(8,128)(2,1)} %get-tuple-element.21) | copy-start | bytes 786436
  58.2 2.4 %copy-start.1 = (bf16[512,256]{1,0:T(8,128)(2,1)S(1)}, bf16[512,256]{1,0:T(8,128)(2,1)}, u32[]{:S(2)}) copy-start(bf16[512,256]{1,0:T(8,128)(2,1)} %get-tuple-element.22) | copy-start | bytes 786436
  59.9 2.0 %copy-start = (f32[512,256]{1,0:T(8,128)S(1)}, f32[512,256]{1,0:T(8,128)}, u32[]{:S(2)}) copy-start(f32[512,256]{1,0:T(8,128)} %get-tuple-element.24) | copy-start | bytes 1572868
  60.6 0.7 %copy-start.3 = (f32[1,256]{1,0:T(1,128)S(1)}, f32[1,256]{1,0:T(1,128)}, u32[]{:S(2)}) copy-start(f32[1,256]{1,0:T(1,128)} %get-tuple-element.13) | copy-start | bytes 3076
